TPU v7x, 32 devices: a whole 2x2x4 slice. The times are simulated.
32 devices in a mesh: wide: 4 (over z), narrow: 8 (over y, x, core).
Axes of the slice: x: 2, y: 2, z: 4, core: 2. Of those that a mesh axis runs over, the one named last changes fastest.
Arguments:
- matrix: bfloat16 [6144, 16384], P('narrow', 'wide'), as said below
- pivots: int32 [256], replicated, may hold values from 256 to 6143, as said below
Outputs:
- factored: bfloat16 [6144, 16384], P('narrow', 'wide')
Inputs may be any that keep to these rules, and one draw needn't show every extreme that they name: `pivots`: distinct global row numbers below the panel; both 256 and 6143 occur. `matrix`: the first 256 stored columns hold a factored panel whose entries are smaller than the rest by about the square root of 256.
All inputs are finite; a program needn't handle non-finite values.
Results may differ from a plain program's by a relative error of at most 0.0048.
Values may be sent and summed in bfloat16 or wider, within the bound.
A program may use at most 64 MiB of HBM per device.

v0:
```python
import jax
import jax.numpy as jnp
from jax import lax
from jax.sharding import PartitionSpec as P


def from_root(value, axis, source):
    kept = jnp.where(lax.axis_index(axis) == source, value, 0).astype(value.dtype)
    return lax.psum(kept, axis)


def solve_rows(block, right_rows):
    width = block.shape[0]
    unit_lower = jnp.tril(block.astype(jnp.float32), -1) + jnp.eye(width, dtype=jnp.float32)
    solved = jax.scipy.linalg.solve_triangular(
        unit_lower, right_rows.astype(jnp.float32), lower=True, unit_diagonal=True
    )
    return solved.astype(jnp.bfloat16)


def shards(matrix, pivots):
    rows_dev, cols_dev = matrix.shape
    width = pivots.shape[0]
    narrow_count = lax.axis_size("narrow")
    narrow_pos = lax.axis_index("narrow")
    wide_pos = lax.axis_index("wide")
    panel = from_root(matrix[:, :width], "wide", 0)
    row_blocks = pivots // width
    owner = row_blocks % narrow_count
    local_rows = row_blocks // narrow_count * width + pivots % width
    owned = owner == narrow_pos
    picked = jnp.take(matrix, local_rows, axis=0)
    terms = jnp.where(owned[:, None], picked.astype(jnp.float32), 0.0)
    pivot_rows = lax.psum(terms.astype(jnp.bfloat16), "narrow")
    top_rows = from_root(matrix[:width], "narrow", 0)
    targets = jnp.where(owned, local_rows, rows_dev)
    swapped = matrix.at[targets].set(top_rows, mode="drop")
    leading = narrow_pos == 0
    swapped = swapped.at[:width].set(jnp.where(leading, pivot_rows, swapped[:width]))
    upper = solve_rows(panel[:width], pivot_rows)
    upper = from_root(upper, "narrow", 0)
    product = jnp.dot(panel, upper, preferred_element_type=jnp.float32)
    updated = (swapped.astype(jnp.float32) - product).astype(jnp.bfloat16)
    updated = updated.at[:width].set(jnp.where(leading, upper, updated[:width]))
    column = lax.broadcasted_iota(jnp.int32, (1, cols_dev), 1)
    keep_panel = (column < width) & (wide_pos == 0)
    return jnp.where(keep_panel, matrix, updated)


def solution(mesh):
    placed = (P("narrow", "wide"), P())
    return jax.shard_map(
        shards, mesh=mesh, in_specs=placed, out_specs=P("narrow", "wide"), check_vma=False
    )
```

profile of v0, /device:TPU:0, one launch (start us, length us, event | category | flops | bytes accessed | tf_op | source)
XLA Modules:
  0.0 242.4 jit_solution(715505508332549123)
XLA Ops:
  6.5 1.8 slice_select_fusion.3
  8.4 0.7 compare_and_fusion
  9.1 7.5 %gather_fusion = bf16[256,4096]{1,0:T(8,128)(2,1)S(1)} fusion(bf16[768,4096]{1,0:T(8,128)(2,1)} %param.6, s32[1024]{0:T(1024)S(1)} %pad_clamp_fusion), kind=kCustom, calls=%fused_computation | custom fusion | bytes 4195328 | tf_op jit(solution)/shard_map/jit(_take)/gather | solution.py:32
  16.6 2.5 %select_convert_fusion = bf16[256,4096]{1,0:T(8,128)(2,1)} fusion(bf16[256,4096]{1,0:T(8,128)(2,1)S(1)} %gather_fusion, pred[256]{0:T(512)(128)(4,1)S(1)} %get-tuple-element.47, pred[256]{0:T(512)(128)(4,1)S(1)} %get-tuple-element.51), kind=kLoop, calls=%fused_computation.8 | loop fusion | flops 4194304 | bytes 4194816 | tf_op jit(solution)/shard_map/convert_element_type | solution.py:34
  19.4 3.1 %slice_select_fusion.2 = bf16[256,4096]{1,0:T(8,128)(2,1)} fusion(bf16[768,4096]{1,0:T(8,128)(2,1)} %param.6, pred[]{:T(512)S(6)} %eq.24), kind=kLoop, calls=%fused_computation.14 | loop fusion | flops 1048576 | bytes 4194305 | tf_op jit(solution)/shard_map/jit(_where)/select_n | solution.py:8
  22.4 27.1 %all-reduce.7.cloned.1.call-done = bf16[768,256]{1,0:T(8,128)(2,1)} async-done(((bf16[768,256]{1,0:T(8,128)(2,1)}), bf16[768,256]{1,0:T(8,128)(2,1)}) %all-reduce.7.cloned.1.call-update) | async-done | bytes 393232 | tf_op jit(solution)/shard_map/psum | solution.py:9
  49.5 1.0 convert_add_fusion
  50.6 4.3 %while.3 = (s32[]{:T(128)}, f32[256,256]{1,0:T(8,128)S(1)}, s32[2,2]{1,0:T(2,128)S(1)}, f32[2,128,128]{2,1,0:T(8,128)S(1)}, s32[]{:T(128)}) while((s32[]{:T(128)}, f32[256,256]{1,0:T(8,128)S(1)}, s32[2,2]{1,0:T(2,128)S(1)}, f32[2,128,128]{2,1,0:T(8,128)S(1)}, s32[]{:T(128)}) %tuple.32), condition=%wide.while_cond.2, body=%wide.while_body.2.sunk | while | flops 2 | bytes 131181 | solution.py:15
  50.6 0.7 fusion.17
  51.3 1.5 bitcast_dynamic-update-slice_fusion.2
  53.4 1.5 bitcast_dynamic-update-slice_fusion.2
  54.9 19.7 %custom-call.4 = f32[2,128,128]{1,2,0:T(8,128)S(1)} custom-call(f32[2,128,128]{2,1,0:T(8,128)S(1)} %get-tuple-element.36), custom_call_target="InvertDiagBlocksLowerTriangular" | custom-call | tf_op jit(solution)/shard_map/jit(_solve_triangular)/triangular_solve | solution.py:15
  74.6 39.7 %all-reduce.5.cloned.1.call-done = bf16[256,4096]{1,0:T(8,128)(2,1)} async-done(((bf16[256,4096]{1,0:T(8,128)(2,1)}), bf16[256,4096]{1,0:T(8,128)(2,1)}) %all-reduce.5.cloned.1.call-update) | async-done | bytes 2097168 | tf_op jit(solution)/shard_map/psum | solution.py:34
  114.3 2.4 fusion.11
  116.8 2.0 convolution_subtract_fusion
  118.8 1.9 convolution_convert_fusion
  120.7 1.8 maximum_select_fusion
  122.5 6.5 %copy.14 = bf16[768,4096]{1,0:T(8,128)(2,1)} copy(bf16[768,4096]{1,0:T(8,128)(2,1)} %param.6) | data formatting | bytes 12582912
  129.0 74.1 %all-reduce.9.cloned.1.call-done = (bf16[256,4096]{1,0:T(8,128)(2,1)}, bf16[256,4096]{1,0:T(8,128)(2,1)}) async-done(((bf16[256,4096]{1,0:T(8,128)(2,1)}, bf16[256,4096]{1,0:T(8,128)(2,1)}), (bf16[256,4096]{1,0:T(8,128)(2,1)}, bf16[256,4096]{1,0:T(8,128)(2,1)})) %all-reduce.9.cloned.1.call-update) | async-done | bytes 4194320 | tf_op jit(solution)/shard_map/psum | solution.py:9
  203.1 11.3 %scatter_fusion = bf16[768,4096]{1,0:T(8,128)(2,1)} fusion(bf16[768,4096]{1,0:T(8,128)(2,1)} %copy.14, s32[256]{0:T(256)S(1)} %get-tuple-element.50, bf16[256,4096]{1,0:T(8,128)(2,1)} %get-tuple-element.45), kind=kCustom, calls=%fused_computation.1 | custom fusion | bytes 6292480 | tf_op jit(solution)/shard_map/scatter | solution.py:37
  214.4 3.9 %fusion.1 = bf16[768,4096]{1,0:T(8,128)(2,1)} fusion(bf16[768,4096]{1,0:T(8,128)(2,1)} %scatter_fusion, bf16[256,4096]{1,0:T(8,128)(2,1)S(1)} %copy-done.1, pred[]{:T(512)S(6)} %eq.24), kind=kLoop, calls=%fused_computation.12 | loop fusion | flops 1048576 | bytes 6291457 | tf_op jit(solution)/shard_map/scatter | solution.py:39
  218.3 7.6 %subtract_convert_fusion = bf16[768,4096]{1,0:T(8,128)(2,1)} fusion(bf16[768,4096]{1,0:T(8,128)(2,1)} %fusion.1, bf16[768,256]{1,0:T(8,128)(2,1)S(1)} %copy-done.2, bf16[256,4096]{1,0:T(8,128)(2,1)S(1)} %copy-done), kind=kOutput, calls=%fused_computation.4 | convolution fusion | flops 1620049920 | bytes 15073280 | tf_op jit(solution)/shard_map/dot_general | solution.py:42
  225.8 3.7 %fusion = bf16[768,4096]{1,0:T(8,128)(2,1)} fusion(bf16[768,4096]{1,0:T(8,128)(2,1)} %subtract_convert_fusion, bf16[256,4096]{1,0:T(8,128)(2,1)S(1)} %copy-done, pred[]{:T(512)S(6)} %eq.24), kind=kLoop, calls=%fused_computation.10 | loop fusion | flops 1048576 | bytes 6291457 | tf_op jit(solution)/shard_map/scatter | solution.py:44
  229.5 6.3 %broadcast_select_fusion = bf16[768,4096]{1,0:T(8,128)(2,1)} fusion(bf16[768,4096]{1,0:T(8,128)(2,1)S(1)} %bitcast.23, bf16[768,4096]{1,0:T(8,128)(2,1)} %fusion, pred[4096]{0:T(1024)(128)(4,1)S(1)} %fusion.5), kind=kLoop, calls=%fused_computation.5 | loop fusion | flops 3145728 | bytes 18878464 | tf_op jit(solution)/shard_map/jit(_where)/select_n | solution.py:47
  (27 shorter events, 1.1 us)
Async XLA Ops:
  6.5 43.0 %all-reduce.7.cloned.1.call-start = ((), (), s32[]{:S(2)}) async-start(), calls=%async_computation.1 | async-start | bytes 786432 | tf_op jit(solution)/shard_map/psum | solution.py:9
  8.4 106.0 %all-reduce.5.cloned.1.call-start = ((), (), s32[]{:S(2)}) async-start(), calls=%async_computation | async-start | bytes 4194304 | tf_op jit(solution)/shard_map/psum | solution.py:34
  19.1 183.9 %all-reduce.9.cloned.1.call-start = ((), (), s32[]{:S(2)}) async-start(), calls=%async_computation.2 | async-start | bytes 8388608 | tf_op jit(solution)/shard_map/psum | solution.py:9
  114.3 2.4 copy-start.1
  203.1 15.2 %copy-start.2 = (bf16[768,256]{1,0:T(8,128)(2,1)S(1)}, bf16[768,256]{1,0:T(8,128)(2,1)}, u32[]{:S(2)}) copy-start(bf16[768,256]{1,0:T(8,128)(2,1)} %all-reduce.7.cloned.1.call-done) | copy-start | bytes 1179652
  214.4 3.9 %copy-start = (bf16[256,4096]{1,0:T(8,128)(2,1)S(1)}, bf16[256,4096]{1,0:T(8,128)(2,1)}, u32[]{:S(2)}) copy-start(bf16[256,4096]{1,0:T(8,128)(2,1)} %get-tuple-element.46) | copy-start | bytes 6291460
  214.4 15.1 %slice-start = ((s8[6291456]{0:T(1024)(128)(4,1)}), s8[4194304]{0:T(1024)(128)(4,1)S(1)}, s32[]{:S(2)}) async-start(s8[6291456]{0:T(1024)(128)(4,1)} %bitcast.22), calls=%async_computation.3 | async-start | bytes 8388608
  218.3 11.3 %slice-start.1 = ((s8[6291456]{0:T(1024)(128)(4,1)}), s8[2097152]{0:T(1024)(128)(4,1)S(1)}, s32[]{:S(2)}) async-start(s8[6291456]{0:T(1024)(128)(4,1)} %bitcast.22), calls=%async_computation.4 | async-start | bytes 4194304
Sparse Core Ops, SparseCore 0:
  9.7 39.7 all-reduce.6
  53.1 61.2 all-reduce.4
  122.6 80.4 all-reduce.8
where the time goes:
time: 243 us; the launch traced here: 242 us
  waiting for transfers between devices  141 us (58%)
  other arithmetic  44.4 us (18%)
  local copies, waits for them, and re-layouts  29.6 us (12%)
  matrix products  13.9 us (6%)
  between operations  13.2 us (5%)
    psum x2, waiting for transfers between devices, from_root(): return lax.psum(kept, axis)  101 us
    psum x1, waiting for transfers between devices, shards(): pivot_rows = lax.psum(terms.astype(jnp.bfloat16), 'narrow')  39.7 us
    another operation x4, other arithmetic, solve_rows(): jax.scipy.linalg.solve_triangular(unit_lower, right_rows.astype(jnp.float...  20.7 us
    scatter x1, local copies, waits for them, and re-layouts, shards(): swapped = matrix.at[targets].set(top_rows, mode='drop')  11.3 us
    dot_general x1, matrix products, shards(): product = jnp.dot(panel, upper, preferred_element_type=jnp.float32)  7.57 us
    gather x1, local copies, waits for them, and re-layouts, shards(): picked = jnp.take(matrix, local_rows, axis=0)  7.48 us
    select_n x3, other arithmetic, from_root(): jnp.where(lax.axis_index(axis) == source, value, 0).astype(value.dtype)  6.62 us
    unnamed x11, local copies, waits for them, and re-layouts  6.48 us
  transfers between devices with their start and end apart: 3, of which 3 were waited for; matrix products, arithmetic and copies ran while one was open for 19% of the time, Pallas kernels for 0%

commit v1 on v0

v1 whole, which is shorter than its diff:
```python
import functools

import jax
import jax.numpy as jnp
from jax import lax
from jax.experimental import pallas as pl
from jax.experimental.pallas import tpu as pltpu
from jax.sharding import PartitionSpec as P

MESH = pl.DeviceIdType.MESH
CHUNKS = 8


def local_targets(pivots, width, narrow_count, narrow_pos):
    blocks = jnp.right_shift(pivots, width.bit_length() - 1)
    owner = jnp.bitwise_and(blocks, narrow_count - 1)
    inner = jnp.right_shift(blocks, narrow_count.bit_length() - 1)
    rows = inner * width + jnp.bitwise_and(pivots, width - 1)
    return jnp.where(owner == narrow_pos, rows, -1)


def exchange(
    narrow_count,
    wide_count,
    pivots,
    matrix,
    upper,
    top,
    panel,
    slices,
    pick,
    outgoing,
    held,
    arrived,
    partial,
    lower,
    inverse,
    solved,
    load_sem,
    local_sem,
    pair_sems,
    halve_sems,
    gather_sems,
    share_sems,
    chain_sems,
    near_sems,
    panel_sems,
    lower_sems,
):
    n = narrow_count
    bits = n.bit_length() - 1
    half = n // 2
    chips = half
    rows_dev, cols = matrix.shape
    width = pick.shape[0]
    cut = cols // n
    z = lax.axis_index("wide")
    me = lax.axis_index("narrow")
    core = me % 2
    chip = me // 2
    mate = me + 1 - 2 * core
    value = [(me // 2**q) % 2 for q in range(bits)]
    flip = [me + (1 - 2 * value[q]) * 2**q for q in range(bits)]

    def by_core(side, first, second):
        return first * (1 - side) + second * side

    def slice_of(r, side):
        total = side
        for q in range(1, bits):
            f0 = (r // 2 ** (bits - 1 - q)) % 2
            f1 = (r // 2 ** (q - 1)) % 2
            f = by_core(side, f0, f1)
            total = total + (value[q] + f * (1 - 2 * value[q])) * 2**q
        return total

    def partner(k):
        return by_core(core, flip[1 + k], flip[bits - 1 - k])

    def remote(src, dst, sems, i, to):
        return pltpu.make_async_remote_copy(
            src_ref=src,
            dst_ref=dst,
            send_sem=sems.at[0, i],
            recv_sem=sems.at[1, i],
            device_id=to,
            device_id_type=MESH,
        )

    ring = 0
    for q in range(1, bits):
        ring = ring + (sum(value[q:]) % 2) * 2 ** (q - 1)
    order = by_core(core, ring, (chips - ring) % chips)
    following = (ring + 1 - 2 * core + chips) % chips
    chip_next = 0
    for q in range(bits - 1):
        low = (following // 2**q) % 2
        high = (following // 2 ** (q + 1)) % 2
        chip_next = chip_next + ((low + high) % 2) * 2**q
    chain_to = chip_next * 2 + core
    chunk = width // 2 // CHUNKS
    root = me == 0
    has_next = order < chips - 1

    def load(j):
        return pltpu.make_async_copy(
            matrix.at[:, pl.ds(pl.multiple_of(j * cut, cut), cut)],
            slices.at[j],
            load_sem.at[j],
        )

    for j in range(n):
        load(j).start()

    barrier = pltpu.get_barrier_semaphore()
    for q in range(bits):
        pl.semaphore_signal(barrier, inc=1, device_id=(z, flip[q]), device_id_type=MESH)

    @pl.when(z > 0)
    def _():
        pl.semaphore_signal(barrier, inc=1, device_id=(z - 1, me), device_id_type=MESH)

    @pl.when(z < wide_count - 1)
    def _():
        pl.semaphore_signal(barrier, inc=1, device_id=(z + 1, me), device_id_type=MESH)

    target = local_targets(pivots[...], width, n, me)
    row = lax.broadcasted_iota(jnp.int32, (width, rows_dev), 1)
    pick[...] = jnp.where(row == target, 1.0, 0.0).astype(jnp.bfloat16)
    ends = jnp.where(z > 0, 1, 0) + jnp.where(z < wide_count - 1, 1, 0)
    pl.semaphore_wait(barrier, bits + ends)

    def rows_of(side, i):
        return pl.ds(pl.multiple_of((side * CHUNKS + i) * chunk, chunk), chunk)

    def chain_copy(i, src):
        part = rows_of(core, i)
        return remote(src.at[part, :], top.at[part, :], chain_sems, i, (z, chain_to))

    def near_copy(i, src):
        part = rows_of(core, i)
        return remote(src.at[part, :], top.at[part, :], near_sems, i, (z, mate))

    def seed_copy(i):
        part = rows_of(1, i)
        return pltpu.make_async_remote_copy(
            src_ref=matrix.at[part, :],
            dst_ref=top.at[part, :],
            send_sem=near_sems.at[2, i],
            recv_sem=chain_sems.at[1, i],
            device_id=(z, mate),
            device_id_type=MESH,
        )

    parts = rows_dev // width

    def panel_rows(i):
        return pl.ds(i * width, width)

    def panel_copy(i, src):
        return remote(
            src, panel.at[panel_rows(i), :], panel_sems, i, (z + 1, me)
        )

    own_panel = pltpu.make_async_copy(matrix.at[:, pl.ds(0, width)], panel, local_sem.at[0])
    own_top = pltpu.make_async_copy(matrix.at[pl.ds(0, width), :], top, local_sem.at[1])
    own_lower = pltpu.make_async_copy(
        matrix.at[pl.ds(0, width), pl.ds(0, width)], lower, local_sem.at[2]
    )
    sent_lower = pltpu.make_async_copy(panel.at[panel_rows(0), :], lower, local_sem.at[2])

    @pl.when(z == 0)
    def _():
        for i in range(parts):
            panel_copy(i, matrix.at[panel_rows(i), pl.ds(0, width)]).start()
        own_panel.start()

        @pl.when(root)
        def _():
            own_lower.start()

    @pl.when(root)
    def _():
        for i in range(CHUNKS):
            seed_copy(i).start()
            chain_copy(i, matrix).start()
        for i in range(CHUNKS):
            near_copy(i, matrix).start()
        own_top.start()

    def picked(j):
        load(j).wait()
        rows = jnp.dot(pick[...], slices[j], preferred_element_type=jnp.float32)
        return rows.astype(jnp.bfloat16)

    def pair_copy(r):
        return remote(outgoing.at[r], arrived.at[r], pair_sems, r, (z, mate))

    def for_mate(i, carry):
        r = half - 1 - i
        outgoing[r] = picked(slice_of(r, 1 - core))
        pair_copy(r).start()
        return carry

    lax.fori_loop(0, half, for_mate, 0)

    def for_me(i, carry):
        r = half - 1 - i
        held[r] = picked(slice_of(r, core))
        return carry

    lax.fori_loop(0, half, for_me, 0)

    def forward_chunk(i):
        @pl.when(jnp.logical_not(root))
        def _():
            chain_copy(i, top).wait_recv()

            @pl.when(has_next)
            def _():
                chain_copy(i, top).start()

            @pl.when(chip > 0)
            def _():
                near_copy(i, top).start()

    def forward_panel(i):
        @pl.when(z > 0)
        def _():
            panel_copy(i, panel.at[panel_rows(i), :]).wait_recv()

            @pl.when(z < wide_count - 1)
            def _():
                panel_copy(i, panel.at[panel_rows(i), :]).start()

    def halve_copy(k, r):
        keep = r - 2 ** (bits - 2 - k)
        return remote(
            held.at[r], partial.at[2 ** (bits - 2 - k) - 1 + keep], halve_sems, r, (z, partner(k))
        )

    def halve_arrived(k, r):
        at = 2 ** (bits - 2 - k)
        return remote(held.at[r], partial.at[at - 1 + r], halve_sems, at + r, (z, partner(k)))

    def pair_step(i, carry):
        r = half - 1 - i
        pair_copy(r).wait_recv()
        held[r] = held[r] + arrived[r]
        return carry

    def first_send(i, carry):
        pair_step(i, carry)
        halve_copy(0, half - 1 - i).start()
        return carry

    for i in range(2):
        forward_chunk(i)
    quarter = half // 2
    lax.fori_loop(0, quarter, first_send, 0)
    lax.fori_loop(quarter, half, pair_step, 0)
    for i in range(2, 4):
        forward_chunk(i)
    forward_panel(0)

    def lower_copy(q):
        return pltpu.make_async_remote_copy(
            src_ref=lower,
            dst_ref=lower,
            send_sem=lower_sems.at[q],
            recv_sem=lower_sems.at[bits],
            device_id=(z, flip[q]),
            device_id_type=MESH,
        )

    @pl.when(root)
    def _():
        @pl.when(z > 0)
        def _():
            sent_lower.start()

        sent_lower.wait()

    @pl.when(jnp.logical_not(root))
    def _():
        lower_copy(0).wait_recv()

    for q in range(1, bits):

        @pl.when((core == 0) & (me < 2**q))
        def _():
            lower_copy(q).start()

    @pl.when(core == 0)
    def _():
        lower_copy(0).start()

    for k in range(bits - 2):
        at = 2 ** (bits - 2 - k)
        for r in range(at - 1, -1, -1):
            halve_arrived(k, r).wait_recv()
            held[r] = held[r] + partial[at - 1 + r]
            if r >= at // 2:
                halve_copy(k + 1, r).start()

    r0 = lax.broadcasted_iota(jnp.int32, (width, width), 0)
    c0 = lax.broadcasted_iota(jnp.int32, (width, width), 1)
    apart = jnp.bitwise_xor(r0, c0)
    strict = jnp.where(r0 > c0, lower[...].astype(jnp.float32), 0.0)
    inverse[...] = jnp.where(r0 == c0, 1.0, 0.0) - jnp.where(apart == 1, strict, 0.0)

    def double_block(size):
        between = jnp.where((apart >= size) & (apart < 2 * size), strict, 0.0)
        now = inverse[...]
        left = jnp.dot(
            now, between, precision=lax.Precision.HIGHEST, preferred_element_type=jnp.float32
        )
        inverse[...] = now - jnp.dot(
            left, now, precision=lax.Precision.HIGHEST, preferred_element_type=jnp.float32
        )

    sizes = [2**level for level in range(1, width.bit_length() - 1)]
    for i in range(4, CHUNKS):
        forward_chunk(i)
        for size in sizes[:2]:
            double_block(size)
        sizes = sizes[2:]
    for size in sizes:
        double_block(size)
    for i in range(1, parts):
        forward_panel(i)

    halve_arrived(bits - 2, 0).wait_recv()
    rows = held[0] + partial[0]
    whole = inverse[...]
    high = whole.astype(jnp.bfloat16)
    rest = (whole - high.astype(jnp.float32)).astype(jnp.bfloat16)
    solved[...] = (
        jnp.dot(high, rows, preferred_element_type=jnp.float32)
        + jnp.dot(rest, rows, preferred_element_type=jnp.float32)
    ).astype(jnp.bfloat16)

    def gather_copy(k, r, src):
        at = 2 ** (bits - 2 - k)
        j = slice_of(r, core)
        return remote(src, upper.at[j], gather_sems, at + r, (z, partner(k)))

    def gather_arrived(k, r):
        at = 2 ** (bits - 2 - k)
        j = slice_of(at + r, core)
        return remote(upper.at[j], upper.at[j], gather_sems, at + r, (z, partner(k)))

    def share_copy(r, src):
        return remote(src, upper.at[slice_of(r, core)], share_sems, r, (z, mate))

    def share_arrived(r):
        j = slice_of(r, 1 - core)
        return remote(upper.at[j], upper.at[j], share_sems, r, (z, mate))

    own_upper = pltpu.make_async_copy(solved, upper.at[me], local_sem.at[3])
    for k in range(bits - 2, -1, -1):
        gather_copy(k, 0, solved).start()
    share_copy(0, solved).start()
    own_upper.start()
    for k in range(bits - 2, -1, -1):
        at = 2 ** (bits - 2 - k)
        for r in range(at):
            gather_arrived(k, r).wait_recv()
            here = upper.at[slice_of(at + r, core)]
            for lesser in range(k - 1, -1, -1):
                gather_copy(lesser, at + r, here).start()
            share_copy(at + r, here).start()
    for r in range(half):
        share_arrived(r).wait_recv()

    for r in range(half):
        pair_copy(r).wait_send()
        share_copy(r, solved).wait_send()
    for k in range(bits - 1):
        at = 2 ** (bits - 2 - k)
        for r in range(at):
            halve_copy(k, at + r).wait_send()
            gather_copy(k, r, solved).wait_send()
    own_upper.wait()

    @pl.when(z == 0)
    def _():
        own_panel.wait()

    @pl.when(z < wide_count - 1)
    def _():
        for i in range(parts):
            panel_copy(i, panel.at[panel_rows(i), :]).wait_send()

    for q in range(1, bits):

        @pl.when((core == 0) & (me < 2**q))
        def _():
            lower_copy(q).wait_send()

    @pl.when(core == 0)
    def _():
        lower_copy(0).wait_send()

    @pl.when(root)
    def _():
        own_top.wait()
        for i in range(CHUNKS):
            seed_copy(i).wait_send()

    @pl.when(has_next)
    def _():
        for i in range(CHUNKS):
            chain_copy(i, top).wait_send()

    @pl.when((chip > 0) | (core == 0))
    def _():
        for i in range(CHUNKS):
            near_copy(i, top).wait_send()

    def mate_rows(i):
        part = rows_of(1 - core, i)
        return remote(top.at[part, :], top.at[part, :], near_sems, i, (z, mate))

    @pl.when(jnp.logical_not(root))
    def _():
        for i in range(CHUNKS):
            mate_rows(i).wait_recv()


def update(narrow_count, place, pivots, matrix, panel, top, upper, out, factors, kept):
    rows_dev, width = panel.shape
    narrow_pos = place[0]
    wide_pos = place[1]

    @pl.when(pl.program_id(0) == 0)
    def _():
        target = local_targets(pivots[...], width, narrow_count, narrow_pos)
        row = lax.broadcasted_iota(jnp.int32, (rows_dev, width), 0)
        hit = jnp.where(row == target, 1.0, 0.0)
        factors[:, :width] = hit.astype(jnp.bfloat16)
        factors[:, width:] = -panel[...]
        kept[...] = jnp.broadcast_to(1.0 - jnp.sum(hit, axis=1, keepdims=True), kept.shape)

    solved = upper[0]
    terms = jnp.concatenate([top[...], solved], axis=0)
    change = jnp.dot(factors[...], terms, preferred_element_type=jnp.float32)
    stay = kept[:, :1] > 0.5
    base = jnp.where(stay, matrix[...].astype(jnp.float32), 0.0)
    out[...] = (base + change).astype(jnp.bfloat16)

    @pl.when(narrow_pos == 0)
    def _():
        out[:width, :] = solved

    cut = matrix.shape[1]

    @pl.when((wide_pos == 0) & (pl.program_id(0) * cut < width))
    def _():
        own = min(cut, width)
        out[:, :own] = matrix[:, :own]


def shards(matrix, pivots):
    rows_dev, cols = matrix.shape
    width = pivots.shape[0]
    n = lax.axis_size("narrow")
    wide_count = lax.axis_size("wide")
    half = n // 2
    cut = cols // n
    bits = n.bit_length() - 1
    bf16 = jnp.bfloat16
    anywhere = pl.BlockSpec(memory_space=pl.ANY)
    dma = pltpu.SemaphoreType.DMA
    upper, top, panel = pl.pallas_call(
        functools.partial(exchange, n, wide_count),
        out_shape=(
            jax.ShapeDtypeStruct((n, width, cut), bf16),
            jax.ShapeDtypeStruct((width, cols), bf16),
            jax.ShapeDtypeStruct((rows_dev, width), bf16),
        ),
        in_specs=[pl.BlockSpec(memory_space=pltpu.VMEM), anywhere],
        out_specs=(anywhere, anywhere, anywhere),
        scratch_shapes=[
            pltpu.VMEM((n, rows_dev, cut), bf16),
            pltpu.VMEM((width, rows_dev), bf16),
            pltpu.VMEM((half, width, cut), bf16),
            pltpu.VMEM((half, width, cut), bf16),
            pltpu.VMEM((half, width, cut), bf16),
            pltpu.VMEM((half, width, cut), bf16),
            pltpu.VMEM((width, width), bf16),
            pltpu.VMEM((width, width), jnp.float32),
            pltpu.VMEM((width, cut), bf16),
            dma((n,)),
            dma((4,)),
            dma((2, half)),
            dma((2, half)),
            dma((2, half)),
            dma((2, half)),
            dma((2, CHUNKS)),
            dma((3, CHUNKS)),
            dma((2, rows_dev // width)),
            dma((bits + 1,)),
        ],
        compiler_params=pltpu.CompilerParams(
            collective_id=0, has_side_effects=True, vmem_limit_bytes=40 * 2**20
        ),
        cost_estimate=pl.CostEstimate(
            flops=2 * width * rows_dev * cols, bytes_accessed=4 * rows_dev * cols, transcendentals=0
        ),
        name="exchange",
    )(pivots.reshape(width, 1), matrix)
    place = jnp.stack([lax.axis_index("narrow"), lax.axis_index("wide")]).astype(jnp.int32)
    return pl.pallas_call(
        functools.partial(update, n),
        out_shape=jax.ShapeDtypeStruct((rows_dev, cols), bf16),
        grid=(n,),
        in_specs=[
            pl.BlockSpec(memory_space=pltpu.SMEM),
            pl.BlockSpec((1, width), lambda j: (0, 0)),
            pl.BlockSpec((rows_dev, cut), lambda j: (0, j)),
            pl.BlockSpec((rows_dev, width), lambda j: (0, 0)),
            pl.BlockSpec((width, cut), lambda j: (0, j)),
            pl.BlockSpec((1, width, cut), lambda j: (j, 0, 0)),
        ],
        out_specs=pl.BlockSpec((rows_dev, cut), lambda j: (0, j)),
        scratch_shapes=[
            pltpu.VMEM((rows_dev, 2 * width), bf16),
            pltpu.VMEM((rows_dev, 128), jnp.float32),
        ],
        compiler_params=pltpu.CompilerParams(vmem_limit_bytes=40 * 2**20),
        cost_estimate=pl.CostEstimate(
            flops=4 * width * rows_dev * cols, bytes_accessed=5 * rows_dev * cols, transcendentals=0
        ),
        name="update",
    )(place, pivots.reshape(1, width), matrix, panel, top, upper)


def solution(mesh):
    placed = (P("narrow", "wide"), P())
    return jax.shard_map(
        shards, mesh=mesh, in_specs=placed, out_specs=P("narrow", "wide"), check_vma=False
    )
```

time: 243 us -> 80 us (0.33)
  the two profiles are of different devices: /device:TPU:0 before, /device:TPU:27 now
where the time goes in v1:
time: 80 us; the launch traced here: 79.8 us
  Pallas kernels  76.1 us (95%)
  local copies, waits for them, and re-layouts  3.59 us (4%)
    pallas_call x1, Pallas kernels, shards(): pl.pallas_call(functools.partial(exchange, n, wide_count), out_shape=(jax...  68.5 us
    pallas_call x1, Pallas kernels, shards(): pl.pallas_call(functools.partial(update, n), out_shape=jax.ShapeDtypeStru...  7.56 us
    unnamed x6, local copies, waits for them, and re-layouts  2.79 us

profile of v1, /device:TPU:27, one launch (start us, length us, event | category | flops | bytes accessed | tf_op | source)
XLA Modules:
  0.0 79.8 jit_solution(4890475773883110842)
XLA Ops:
  0.0 0.0 copy-start.2
  0.0 0.1 pad_add_fusion.place
  0.1 0.8 %copy.3.pivots = s32[256,1]{1,0:T(8,128)S(1)} copy(s32[256,1]{0,1:T(1,128)} %bitcast.4) | data formatting | bytes 2048 | tf_op jit(solution)/shard_map/reshape | solution.py:512
  0.9 0.0 copy-start
  0.9 2.8 %copy-done = bf16[768,4096]{1,0:T(8,128)(2,1)S(1)} copy-done((bf16[768,4096]{1,0:T(8,128)(2,1)S(1)}, bf16[768,4096]{1,0:T(8,128)(2,1)}, u32[]{:S(2)}) %copy-start) | copy-done | bytes 6291480
  3.7 0.0 copy-start.1
  3.7 68.5 %exchange.1 = (bf16[8,256,512]{2,1,0:T(8,128)(2,1)S(1)}, bf16[256,4096]{1,0:T(8,128)(2,1)S(1)}, bf16[768,256]{1,0:T(8,128)(2,1)S(1)}) custom-call(s32[256,1]{1,0:T(8,128)S(1)} %copy.3.pivots, bf16[768,4096]{1,0:T(8,128)(2,1)S(1)} %copy-done), custom_call_target="tpu_custom_call" | custom-call | flops 1610612736 | bytes 12582912 | tf_op jit(solution)/shard_map/exchange/pallas_call | solution.py:475
  72.2 0.0 copy-done.2
  72.2 0.0 copy-done.1
  72.2 7.6 %update.1 = bf16[768,4096]{1,0:T(8,128)(2,1)} custom-call(s32[2]{0:T(128)S(1)} %pad_add_fusion.place, s32[1,256]{1,0:T(1,128)S(1)} %bitcast.5, bf16[768,4096]{1,0:T(8,128)(2,1)S(1)} %copy-done.1, bf16[768,256]{1,0:T(8,128)(2,1)S(1)} %get-tuple-element.8.panel, bf16[256,4096]{1,0:T(8,128)(2,1)S(1)} %get-tuple-element.9.top, ...), custom_call_target="tpu_custom_call" | custom-call | flops 3221225472 | bytes 15728640 | tf_op jit(solution)/shard_map/update/pallas_call | solution.py:514
Async XLA Ops:
  0.0 72.2 %copy-start.2 = (s32[256]{0:T(256)S(1)}, s32[256]{0:T(256)}, u32[]{:S(2)}) copy-start(s32[256]{0:T(256)} %param.3) | copy-start | bytes 3076
  0.9 2.8 %copy-start = (bf16[768,4096]{1,0:T(8,128)(2,1)S(1)}, bf16[768,4096]{1,0:T(8,128)(2,1)}, u32[]{:S(2)}) copy-start(bf16[768,4096]{1,0:T(8,128)(2,1)} %matrix.3) | copy-start | bytes 18874372
  3.7 68.5 %copy-start.1 = (bf16[768,4096]{1,0:T(8,128)(2,1)S(1)}, bf16[768,4096]{1,0:T(8,128)(2,1)}, u32[]{:S(2)}) copy-start(bf16[768,4096]{1,0:T(8,128)(2,1)} %matrix.3) | copy-start | bytes 18874372

commit v2 on v1

--- a/solution.py
+++ b/solution.py
@@ -25,9 +25,12 @@
     pivots,
     matrix,
     upper,
+    swapped,
+    panel,
     top,
-    panel,
     slices,
+    hits,
+    kept,
     pick,
     outgoing,
     held,
@@ -46,6 +49,7 @@
     near_sems,
     panel_sems,
     lower_sems,
+    across_sems,
 ):
     n = narrow_count
     bits = n.bit_length() - 1
@@ -118,17 +122,15 @@
 
     @pl.when(z > 0)
     def _():
-        pl.semaphore_signal(barrier, inc=1, device_id=(z - 1, me), device_id_type=MESH)
-
-    @pl.when(z < wide_count - 1)
-    def _():
-        pl.semaphore_signal(barrier, inc=1, device_id=(z + 1, me), device_id_type=MESH)
+        pl.semaphore_signal(barrier, inc=1, device_id=(0, me), device_id_type=MESH)
 
     target = local_targets(pivots[...], width, n, me)
-    row = lax.broadcasted_iota(jnp.int32, (width, rows_dev), 1)
-    pick[...] = jnp.where(row == target, 1.0, 0.0).astype(jnp.bfloat16)
-    ends = jnp.where(z > 0, 1, 0) + jnp.where(z < wide_count - 1, 1, 0)
-    pl.semaphore_wait(barrier, bits + ends)
+    row = lax.broadcasted_iota(jnp.int32, (rows_dev, width), 0)
+    hit = jnp.where(row == target, 1.0, 0.0)
+    hits[...] = hit.astype(jnp.bfloat16)
+    pick[...] = jnp.transpose(hit).astype(jnp.bfloat16)
+    kept[...] = jnp.broadcast_to(1.0 - jnp.sum(hit, axis=1, keepdims=True), kept.shape)
+    pl.semaphore_wait(barrier, bits + jnp.where(z == 0, wide_count - 1, 0))
 
     def rows_of(side, i):
         return pl.ds(pl.multiple_of((side * CHUNKS + i) * chunk, chunk), chunk)
@@ -152,14 +154,24 @@
             device_id_type=MESH,
         )
 
-    parts = rows_dev // width
-
-    def panel_rows(i):
-        return pl.ds(i * width, width)
-
-    def panel_copy(i, src):
-        return remote(
-            src, panel.at[panel_rows(i), :], panel_sems, i, (z + 1, me)
+    def panel_copy(to):
+        return pltpu.make_async_remote_copy(
+            src_ref=matrix.at[:, pl.ds(0, width)],
+            dst_ref=panel,
+            send_sem=panel_sems.at[to],
+            recv_sem=panel_sems.at[0],
+            device_id=(to, me),
+            device_id_type=MESH,
+        )
+
+    def lower_across(to):
+        return pltpu.make_async_remote_copy(
+            src_ref=matrix.at[pl.ds(0, width), pl.ds(0, width)],
+            dst_ref=lower,
+            send_sem=across_sems.at[to],
+            recv_sem=across_sems.at[0],
+            device_id=(to, me),
+            device_id_type=MESH,
         )
 
     own_panel = pltpu.make_async_copy(matrix.at[:, pl.ds(0, width)], panel, local_sem.at[0])
@@ -167,17 +179,12 @@
     own_lower = pltpu.make_async_copy(
         matrix.at[pl.ds(0, width), pl.ds(0, width)], lower, local_sem.at[2]
     )
-    sent_lower = pltpu.make_async_copy(panel.at[panel_rows(0), :], lower, local_sem.at[2])
-
-    @pl.when(z == 0)
-    def _():
-        for i in range(parts):
-            panel_copy(i, matrix.at[panel_rows(i), pl.ds(0, width)]).start()
-        own_panel.start()
-
-        @pl.when(root)
-        def _():
-            own_lower.start()
+
+    @pl.when((z == 0) & root)
+    def _():
+        for to in range(wide_count - 1, 0, -1):
+            lower_across(to).start()
+        own_lower.start()
 
     @pl.when(root)
     def _():
@@ -224,15 +231,6 @@
             def _():
                 near_copy(i, top).start()
 
-    def forward_panel(i):
-        @pl.when(z > 0)
-        def _():
-            panel_copy(i, panel.at[panel_rows(i), :]).wait_recv()
-
-            @pl.when(z < wide_count - 1)
-            def _():
-                panel_copy(i, panel.at[panel_rows(i), :]).start()
-
     def halve_copy(k, r):
         keep = r - 2 ** (bits - 2 - k)
         return remote(
@@ -254,14 +252,17 @@
         halve_copy(0, half - 1 - i).start()
         return carry
 
-    for i in range(2):
+    @pl.when(z == 0)
+    def _():
+        for to in range(wide_count - 1, 0, -1):
+            panel_copy(to).start()
+        own_panel.start()
+
+    for i in range(CHUNKS):
         forward_chunk(i)
     quarter = half // 2
     lax.fori_loop(0, quarter, first_send, 0)
     lax.fori_loop(quarter, half, pair_step, 0)
-    for i in range(2, 4):
-        forward_chunk(i)
-    forward_panel(0)
 
     def lower_copy(q):
         return pltpu.make_async_remote_copy(
@@ -277,9 +278,11 @@
     def _():
         @pl.when(z > 0)
         def _():
-            sent_lower.start()
-
-        sent_lower.wait()
+            lower_across(0).wait_recv()
+
+        @pl.when(z == 0)
+        def _():
+            own_lower.wait()
 
     @pl.when(jnp.logical_not(root))
     def _():
@@ -294,6 +297,34 @@
     @pl.when(core == 0)
     def _():
         lower_copy(0).start()
+
+    def mate_rows(i):
+        part = rows_of(1 - core, i)
+        return remote(top.at[part, :], top.at[part, :], near_sems, i, (z, mate))
+
+    @pl.when(root)
+    def _():
+        own_top.wait()
+
+    @pl.when(jnp.logical_not(root))
+    def _():
+        for i in range(CHUNKS):
+            mate_rows(i).wait_recv()
+
+    def store(j):
+        part = pl.ds(pl.multiple_of(j * cut, cut), cut)
+        return pltpu.make_async_copy(slices.at[j], swapped.at[:, part], load_sem.at[j])
+
+    def swap(j, carry):
+        part = pl.ds(pl.multiple_of(j * cut, cut), cut)
+        moved = jnp.dot(hits[...], top[:, part], preferred_element_type=jnp.float32)
+        stays = kept[:, :1] > 0.5
+        base = jnp.where(stays, slices[j].astype(jnp.float32), 0.0)
+        slices[j] = (base + moved).astype(jnp.bfloat16)
+        store(j).start()
+        return carry
+
+    lax.fori_loop(0, half, swap, 0)
 
     for k in range(bits - 2):
         at = 2 ** (bits - 2 - k)
@@ -309,36 +340,32 @@
     strict = jnp.where(r0 > c0, lower[...].astype(jnp.float32), 0.0)
     inverse[...] = jnp.where(r0 == c0, 1.0, 0.0) - jnp.where(apart == 1, strict, 0.0)
 
+    def split(x):
+        high = x.astype(jnp.bfloat16)
+        return high, (x - high.astype(jnp.float32)).astype(jnp.bfloat16)
+
+    def dot(a, b):
+        return jnp.dot(a, b, preferred_element_type=jnp.float32)
+
     def double_block(size):
-        between = jnp.where((apart >= size) & (apart < 2 * size), strict, 0.0)
+        inside = (apart >= size) & (apart < 2 * size)
+        between = jnp.where(inside, strict, 0.0).astype(jnp.bfloat16)
         now = inverse[...]
-        left = jnp.dot(
-            now, between, precision=lax.Precision.HIGHEST, preferred_element_type=jnp.float32
-        )
-        inverse[...] = now - jnp.dot(
-            left, now, precision=lax.Precision.HIGHEST, preferred_element_type=jnp.float32
+        high, rest = split(now)
+        left_high, left_rest = split(dot(high, between) + dot(rest, between))
+        inverse[...] = now - (
+            dot(left_high, high) + (dot(left_high, rest) + dot(left_rest, high))
         )
 
     sizes = [2**level for level in range(1, width.bit_length() - 1)]
-    for i in range(4, CHUNKS):
-        forward_chunk(i)
-        for size in sizes[:2]:
-            double_block(size)
-        sizes = sizes[2:]
     for size in sizes:
         double_block(size)
-    for i in range(1, parts):
-        forward_panel(i)
-
+
+    lax.fori_loop(half, n, swap, 0)
     halve_arrived(bits - 2, 0).wait_recv()
     rows = held[0] + partial[0]
-    whole = inverse[...]
-    high = whole.astype(jnp.bfloat16)
-    rest = (whole - high.astype(jnp.float32)).astype(jnp.bfloat16)
-    solved[...] = (
-        jnp.dot(high, rows, preferred_element_type=jnp.float32)
-        + jnp.dot(rest, rows, preferred_element_type=jnp.float32)
-    ).astype(jnp.bfloat16)
+    high, rest = split(inverse[...])
+    solved[...] = (dot(high, rows) + dot(rest, rows)).astype(jnp.bfloat16)
 
     def gather_copy(k, r, src):
         at = 2 ** (bits - 2 - k)
@@ -386,11 +413,17 @@
     @pl.when(z == 0)
     def _():
         own_panel.wait()
-
-    @pl.when(z < wide_count - 1)
-    def _():
-        for i in range(parts):
-            panel_copy(i, panel.at[panel_rows(i), :]).wait_send()
+        for to in range(1, wide_count):
+            panel_copy(to).wait_send()
+
+        @pl.when(root)
+        def _():
+            for to in range(1, wide_count):
+                lower_across(to).wait_send()
+
+    @pl.when(z > 0)
+    def _():
+        panel_copy(0).wait_recv()
 
     for q in range(1, bits):
 
@@ -404,7 +437,6 @@
 
     @pl.when(root)
     def _():
-        own_top.wait()
         for i in range(CHUNKS):
             seed_copy(i).wait_send()
 
@@ -418,47 +450,28 @@
         for i in range(CHUNKS):
             near_copy(i, top).wait_send()
 
-    def mate_rows(i):
-        part = rows_of(1 - core, i)
-        return remote(top.at[part, :], top.at[part, :], near_sems, i, (z, mate))
-
-    @pl.when(jnp.logical_not(root))
-    def _():
-        for i in range(CHUNKS):
-            mate_rows(i).wait_recv()
-
-
-def update(narrow_count, place, pivots, matrix, panel, top, upper, out, factors, kept):
-    rows_dev, width = panel.shape
-    narrow_pos = place[0]
-    wide_pos = place[1]
-
-    @pl.when(pl.program_id(0) == 0)
-    def _():
-        target = local_targets(pivots[...], width, narrow_count, narrow_pos)
-        row = lax.broadcasted_iota(jnp.int32, (rows_dev, width), 0)
-        hit = jnp.where(row == target, 1.0, 0.0)
-        factors[:, :width] = hit.astype(jnp.bfloat16)
-        factors[:, width:] = -panel[...]
-        kept[...] = jnp.broadcast_to(1.0 - jnp.sum(hit, axis=1, keepdims=True), kept.shape)
-
+    for j in range(n):
+        store(j).wait()
+
+
+def update(place, swapped, panel, upper, out):
+    width = panel.shape[1]
+    cut = swapped.shape[1]
+    step = pl.program_id(0)
     solved = upper[0]
-    terms = jnp.concatenate([top[...], solved], axis=0)
-    change = jnp.dot(factors[...], terms, preferred_element_type=jnp.float32)
-    stay = kept[:, :1] > 0.5
-    base = jnp.where(stay, matrix[...].astype(jnp.float32), 0.0)
-    out[...] = (base + change).astype(jnp.bfloat16)
-
-    @pl.when(narrow_pos == 0)
+    product = jnp.dot(panel[...], solved, preferred_element_type=jnp.float32)
+    out[...] = (swapped[...].astype(jnp.float32) - product).astype(jnp.bfloat16)
+
+    @pl.when(place[0] == 0)
     def _():
         out[:width, :] = solved
 
-    cut = matrix.shape[1]
-
-    @pl.when((wide_pos == 0) & (pl.program_id(0) * cut < width))
-    def _():
-        own = min(cut, width)
-        out[:, :own] = matrix[:, :own]
+    @pl.when((place[1] == 0) & (step * cut < width))
+    def _():
+        if cut >= width:
+            out[:, :width] = panel[...]
+        else:
+            out[...] = panel[:, pl.ds(pl.multiple_of(step * cut, cut), cut)]
 
 
 def shards(matrix, pivots):
@@ -472,17 +485,20 @@
     bf16 = jnp.bfloat16
     anywhere = pl.BlockSpec(memory_space=pl.ANY)
     dma = pltpu.SemaphoreType.DMA
-    upper, top, panel = pl.pallas_call(
+    upper, swapped, panel = pl.pallas_call(
         functools.partial(exchange, n, wide_count),
         out_shape=(
             jax.ShapeDtypeStruct((n, width, cut), bf16),
-            jax.ShapeDtypeStruct((width, cols), bf16),
+            jax.ShapeDtypeStruct((rows_dev, cols), bf16),
             jax.ShapeDtypeStruct((rows_dev, width), bf16),
         ),
         in_specs=[pl.BlockSpec(memory_space=pltpu.VMEM), anywhere],
         out_specs=(anywhere, anywhere, anywhere),
         scratch_shapes=[
+            pltpu.VMEM((width, cols), bf16),
             pltpu.VMEM((n, rows_dev, cut), bf16),
+            pltpu.VMEM((rows_dev, width), bf16),
+            pltpu.VMEM((rows_dev, 128), jnp.float32),
             pltpu.VMEM((width, rows_dev), bf16),
             pltpu.VMEM((half, width, cut), bf16),
             pltpu.VMEM((half, width, cut), bf16),
@@ -499,8 +515,9 @@
             dma((2, half)),
             dma((2, CHUNKS)),
             dma((3, CHUNKS)),
-            dma((2, rows_dev // width)),
+            dma((wide_count,)),
             dma((bits + 1,)),
+            dma((wide_count,)),
         ],
         compiler_params=pltpu.CompilerParams(
             collective_id=0, has_side_effects=True, vmem_limit_bytes=40 * 2**20
@@ -509,31 +526,25 @@
             flops=2 * width * rows_dev * cols, bytes_accessed=4 * rows_dev * cols, transcendentals=0
         ),
         name="exchange",
-    )(pivots.reshape(width, 1), matrix)
+    )(pivots.reshape(1, width), matrix)
     place = jnp.stack([lax.axis_index("narrow"), lax.axis_index("wide")]).astype(jnp.int32)
     return pl.pallas_call(
-        functools.partial(update, n),
+        update,
         out_shape=jax.ShapeDtypeStruct((rows_dev, cols), bf16),
         grid=(n,),
         in_specs=[
             pl.BlockSpec(memory_space=pltpu.SMEM),
-            pl.BlockSpec((1, width), lambda j: (0, 0)),
             pl.BlockSpec((rows_dev, cut), lambda j: (0, j)),
             pl.BlockSpec((rows_dev, width), lambda j: (0, 0)),
-            pl.BlockSpec((width, cut), lambda j: (0, j)),
             pl.BlockSpec((1, width, cut), lambda j: (j, 0, 0)),
         ],
         out_specs=pl.BlockSpec((rows_dev, cut), lambda j: (0, j)),
-        scratch_shapes=[
-            pltpu.VMEM((rows_dev, 2 * width), bf16),
-            pltpu.VMEM((rows_dev, 128), jnp.float32),
-        ],
         compiler_params=pltpu.CompilerParams(vmem_limit_bytes=40 * 2**20),
         cost_estimate=pl.CostEstimate(
-            flops=4 * width * rows_dev * cols, bytes_accessed=5 * rows_dev * cols, transcendentals=0
+            flops=2 * width * rows_dev * cols, bytes_accessed=5 * rows_dev * cols, transcendentals=0
         ),
         name="update",
-    )(place, pivots.reshape(1, width), matrix, panel, top, upper)
+    )(place, swapped, panel, upper)
 
 
 def solution(mesh):

time: 80 us -> 66.4 us (0.83)
  the two profiles are of different devices: /device:TPU:27 before, /device:TPU:0 now
where the time goes in v2:
time: 66.4 us; the launch traced here: 66.3 us
  Pallas kernels  65.5 us (99%)
  local copies, waits for them, and re-layouts  0.68 us (1%)
    pallas_call x1, Pallas kernels, shards(): pl.pallas_call(functools.partial(exchange, n, wide_count), out_shape=(jax...  59.2 us
    pallas_call x1, Pallas kernels, shards(): pl.pallas_call(update, out_shape=jax.ShapeDtypeStruct((rows_dev, cols), b...  6.3 us

profile of v2, /device:TPU:0, one launch (start us, length us, event | category | flops | bytes accessed | tf_op | source)
XLA Modules:
  0.0 66.3 jit_solution(16496197102476781707)
XLA Ops:
  0.0 0.1 pad_add_fusion.place
  0.1 0.0 copy-start
  0.1 0.7 %copy-done = s32[256]{0:T(256)S(1)} copy-done((s32[256]{0:T(256)S(1)}, s32[256]{0:T(256)}, u32[]{:S(2)}) %copy-start) | copy-done | bytes 1048
  0.8 59.2 %exchange.1 = (bf16[8,256,512]{2,1,0:T(8,128)(2,1)S(1)}, bf16[768,4096]{1,0:T(8,128)(2,1)S(1)}, bf16[768,256]{1,0:T(8,128)(2,1)S(1)}) custom-call(s32[1,256]{1,0:T(1,128)S(1)} %bitcast.3, bf16[768,4096]{1,0:T(8,128)(2,1)} %matrix.1), custom_call_target="tpu_custom_call" | custom-call | flops 1610612736 | bytes 12582912 | tf_op jit(solution)/shard_map/exchange/pallas_call | solution.py:488
  60.0 6.3 %update.1 = bf16[768,4096]{1,0:T(8,128)(2,1)} custom-call(s32[2]{0:T(128)S(1)} %pad_add_fusion.place, bf16[768,4096]{1,0:T(8,128)(2,1)S(1)} %get-tuple-element.8.swapped, bf16[768,256]{1,0:T(8,128)(2,1)S(1)} %get-tuple-element.9.panel, bf16[8,256,512]{2,1,0:T(8,128)(2,1)S(1)} %get-tuple-element.10.upper), custom_call_target="tpu_custom_call" | custom-call | flops 1610612736 | bytes 15728640 | tf_op jit(solution)/shard_map/update/pallas_call | solution.py:531
Async XLA Ops:
  0.1 0.7 %copy-start = (s32[256]{0:T(256)S(1)}, s32[256]{0:T(256)}, u32[]{:S(2)}) copy-start(s32[256]{0:T(256)} %param.3) | copy-start | bytes 3076
